TPU v7x, 128 devices: a whole 4x4x4 slice. The times are simulated.
128 devices in a mesh: seq: 16 (over x, y), section: 8 (over z, core).
Axes of the slice: x: 4, y: 4, z: 4, core: 2. Of those that a mesh axis runs over, the one named last changes fastest.
Arguments:
- hidden: bfloat16 [8, 6144, 2560], P('section', 'seq'), may hold values from -6 to 6
- query_norm_gain: float32 [8, 2560], P('section'), may hold values from 0.25 to 1.75
- key_norm_gain: float32 [8, 2560], P('section'), may hold values from 0.25 to 1.75
- text_kv: bfloat16 [8, 16, 2, 512, 2560], P('section', 'seq'), may hold values from -6 to 6
- holder: int32 [8], P('section'), may hold values from 0 to 15
- pattern: int32 [48, 7], replicated, may hold values from 0 to 1, as said below
- grad_out: bfloat16 [8, 6144, 2560], P('section', 'seq'), may hold values from -6 to 6
Outputs:
- attended: bfloat16 [8, 6144, 2560], P('section', 'seq')
- upstream: bfloat16 [8, 6144, 2560], P('section', 'seq')
- text_grad: bfloat16 [8, 2, 512, 2560], P('section')
Inputs may be any that keep to these rules, and one draw needn't show every extreme that they name: pattern[b, 3] = 1 for every block b; entries are 0 or 1.
All inputs are finite; a program needn't handle non-finite values.
Results may differ from a plain program's by a relative error of at most 0.0078.
Values may be sent and summed in bfloat16 or wider, within the bound.
A program may use at most 256 MiB of HBM per device.

v0:
```python
import jax
import jax.numpy as jnp
from jax import lax
from jax.sharding import PartitionSpec as P

HDIM = 128
BLK = 128
eps = 1e-06


def extended(cells, sides, width):
    for axis, dim in sides:
        count = lax.axis_size(axis)
        ends = count - 1
        head = lax.slice_in_dim(cells, 0, width, axis=dim)
        tail = lax.slice_in_dim(cells, cells.shape[dim] - width, cells.shape[dim], axis=dim)
        cells = jnp.concatenate(
            [
                lax.ppermute(tail, axis, [(i, (i + 1) % count) for i in range(ends)]),
                cells,
                lax.ppermute(head, axis, [((i + 1) % count, i) for i in range(ends)]),
            ],
            axis=dim,
        )
    return cells


def from_root(block, axis, owner):
    block = jnp.where(lax.axis_index(axis) == owner, block, jnp.zeros_like(block))
    return lax.psum(block, axis)


def shifted(x, axis, by):
    peers = lax.axis_size(axis)
    pairs = [(i, i + by) for i in range(peers) if 0 <= i + by < peers]
    return lax.ppermute(x, axis, pairs)


def norm_forward(hidden_state, norm_gain):
    hidden_float = hidden_state.astype(jnp.float32)
    inverse_root_norm = lax.rsqrt(
        jnp.mean(hidden_float * hidden_float, axis=-1, keepdims=True) + eps
    )
    normalized_input = hidden_float * inverse_root_norm
    return (
        (normalized_input * norm_gain).astype(jnp.bfloat16),
        normalized_input,
        inverse_root_norm,
    )


def norm_backward(upper_bound, norm_gain, normalized_input, inverse_root_norm):
    scaled_input = upper_bound * norm_gain
    return inverse_root_norm * (
        scaled_input
        - normalized_input * jnp.mean(scaled_input * normalized_input, axis=-1, keepdims=True)
    )


def block_mask(pattern, slab, bpd, nslab):
    span = pattern.shape[1]
    rows = lax.dynamic_slice_in_dim(pattern, slab * bpd, bpd, 0)
    first = jnp.arange(bpd, dtype=jnp.int32)[:, None]
    second = jnp.arange(3 * bpd, dtype=jnp.int32)[None, :]
    offset = second - first
    onehot = offset[:, :, None] == jnp.arange(span, dtype=jnp.int32)[None, None, :]
    picked = jnp.sum(jnp.where(onehot, rows[:, None, :], 0), axis=-1)
    globe = slab * bpd - bpd + second
    inside = (globe >= 0) & (globe < nslab * bpd)
    return (picked > 0) & inside


def token_mask(blocks):
    return jnp.repeat(jnp.repeat(blocks, BLK, axis=0), BLK, axis=1)


def divide_heads(x):
    return x.reshape(x.shape[0], x.shape[1] // HDIM, HDIM).transpose(1, 0, 2)


def join_heads(x):
    return x.transpose(1, 0, 2).reshape(x.shape[1], x.shape[0] * x.shape[2])


def query_side(qh, kh, vh, tkh, tvh, doh, attend_mask):
    scale = qh.shape[-1] ** (-0.5)
    keys = jnp.concatenate([kh, tkh], axis=0)
    vals = jnp.concatenate([vh, tvh], axis=0)
    full = jnp.concatenate([attend_mask, jnp.ones((qh.shape[0], tkh.shape[0]), bool)], axis=1)
    scores = jnp.dot(qh, keys.T, preferred_element_type=jnp.float32) * scale
    scores = jnp.where(full, scores, -1e30)
    top = jnp.max(scores, axis=1, keepdims=True)
    total = jnp.sum(jnp.where(full, jnp.exp(scores - top), 0.0), axis=1, keepdims=True)
    lse = top + jnp.log(total)
    probs = jnp.where(full, jnp.exp(scores - lse), 0.0)
    probs_b = probs.astype(jnp.bfloat16)
    out = jnp.dot(probs_b, vals, preferred_element_type=jnp.float32)
    dprob = jnp.dot(doh, vals.T, preferred_element_type=jnp.float32)
    delta = jnp.sum(doh.astype(jnp.float32) * out, axis=1)
    dscore = (probs * (dprob - delta[:, None]) * scale).astype(jnp.bfloat16)
    query_gradient = jnp.dot(dscore, keys, preferred_element_type=jnp.float32)
    dkeys = jnp.dot(dscore.T, qh, preferred_element_type=jnp.float32)
    dvals = jnp.dot(probs_b.T, doh, preferred_element_type=jnp.float32)
    return (out, lse[:, 0], delta, query_gradient, dkeys, dvals)


def local(hidden, query_norm_gain, key_norm_gain, text_kv, holder, pattern, grad_out):
    hidden_state = hidden[0]
    output_gradient = grad_out[0]
    token_rows = hidden_state.shape[0]
    bpd = token_rows // BLK
    slab = lax.axis_index("seq")
    nslab = lax.axis_size("seq")
    normed_query, normalized_input, inverse_root_norm = norm_forward(
        hidden_state, query_norm_gain[0]
    )
    kn, _, _ = norm_forward(hidden_state, key_norm_gain[0])
    near = extended(jnp.stack([kn, hidden_state]), (("seq", 1),), token_rows)
    text_tokens = from_root(text_kv[0, 0], "seq", holder[0])
    attend_mask = token_mask(block_mask(pattern, slab, bpd, nslab))

    def each_head_value(a):
        return query_side(a[0], a[1], a[2], a[3], a[4], a[5], attend_mask)

    saved_residuals = lax.map(
        each_head_value,
        (
            divide_heads(normed_query),
            divide_heads(near[0]),
            divide_heads(near[1]),
            divide_heads(text_tokens[0]),
            divide_heads(text_tokens[1]),
            divide_heads(output_gradient),
        ),
    )
    out, lse, delta, query_gradient, dkeys, dvals = saved_residuals
    ext_rows = 3 * token_rows
    dtext_part = jnp.stack([join_heads(dkeys[:, ext_rows:]), join_heads(dvals[:, ext_rows:])])
    ext = jnp.stack([join_heads(dkeys[:, :ext_rows]), join_heads(dvals[:, :ext_rows])])
    from_upper = shifted(ext[:, :token_rows].astype(jnp.bfloat16), "seq", -1).astype(jnp.float32)
    from_lower = shifted(ext[:, 2 * token_rows :].astype(jnp.bfloat16), "seq", 1).astype(
        jnp.float32
    )
    own_rows = ext[:, token_rows : 2 * token_rows] + from_upper + from_lower
    text_total = lax.psum(dtext_part, "seq")
    grad_hidden = (
        own_rows[1]
        + norm_backward(
            join_heads(query_gradient), query_norm_gain[0], normalized_input, inverse_root_norm
        )
        + norm_backward(own_rows[0], key_norm_gain[0], normalized_input, inverse_root_norm)
    )
    upstream = shifted(grad_hidden.astype(jnp.bfloat16), "section", -1)
    attended = join_heads(out).astype(jnp.bfloat16)
    return (attended[None], upstream[None], text_total.astype(jnp.bfloat16)[None])


def solution(mesh):
    in_specs = (
        P("section", "seq", None),
        P("section", None),
        P("section", None),
        P("section", "seq", None, None, None),
        P("section"),
        P(),
        P("section", "seq", None),
    )
    out_specs = (
        P("section", "seq", None),
        P("section", "seq", None),
        P("section", None, None, None),
    )
    return jax.shard_map(local, mesh=mesh, in_specs=in_specs, out_specs=out_specs, check_vma=False)
```

profile of v0, /device:TPU:24, one launch (start us, length us, event | category | flops | bytes accessed | tf_op | source)
XLA Modules:
  0.0 923.3 jit_solution(16334344849139469414)
XLA Ops:
  7.2 2.8 copy.43
  12.4 2.3 pad_maximum_fusion.9
  14.7 2.6 collective-permute-start.1
  17.4 5.3 collective-permute-start
  23.4 8.0 copy.45
  31.3 2.7 select_bitcast_fusion
  34.7 4.0 copy.46
  38.7 3.2 fusion.42
  41.9 93.5 %collective-permute-done.1 = bf16[2,384,2560]{1,2,0:T(8,128)(2,1)} collective-permute-done((bf16[2,384,2560]{1,2,0:T(8,128)(2,1)}, bf16[2,384,2560]{1,2,0:T(8,128)(2,1)}, u32[]{:S(2)}, u32[]{:S(2)}) %collective-permute-start.1) | collective-permute-done | bytes 3932192 | tf_op jit(solution)/shard_map/ppermute | solution.py:21
  135.4 3.1 collective-permute-done
  138.5 5.1 pad_maximum_fusion.7
  143.7 4.9 fusion.45
  148.6 26.1 %all-reduce.4.cloned.1.call-done = bf16[2,512,2560]{1,2,0:T(8,128)(2,1)} async-done(((bf16[2,512,2560]{1,2,0:T(8,128)(2,1)}), bf16[2,512,2560]{1,2,0:T(8,128)(2,1)}) %all-reduce.4.cloned.1.call-update) | async-done | bytes 5242896 | tf_op jit(solution)/shard_map/psum | solution.py:30
  174.6 5.2 fusion.46
  179.8 351.3 %while.17 = (s32[]{:T(128)}, bf16[20,384,128]{1,2,0:T(8,128)(2,1)}, f32[20,384,128]{1,2,0:T(8,128)}, f32[20,1664,128]{1,2,0:T(8,128)}, f32[20,1664,128]{1,2,0:T(...) while((s32[]{:T(128)}, bf16[20,384,128]{1,2,0:T(8,128)(2,1)}, ...), condition=%wide.region_7.8_spmd.clone, body=%wide.region_3.7_spmd.clone.sunk | while | flops 996523264 | bytes 28792892 | solution.py:125
  192.6 2.5 fusion.70
  203.8 2.3 bitcast_dynamic-update-slice_fusion.2
  210.1 2.6 fusion.70
  227.7 2.5 fusion.70
  238.8 2.3 bitcast_dynamic-update-slice_fusion.2
  245.2 2.6 fusion.70
  262.8 2.5 fusion.70
  273.9 2.3 bitcast_dynamic-update-slice_fusion.2
  280.3 2.5 fusion.70
  291.4 2.3 bitcast_dynamic-update-slice_fusion.2
  297.8 2.6 fusion.70
  309.0 2.3 bitcast_dynamic-update-slice_fusion.2
  315.4 2.5 fusion.70
  326.6 2.3 bitcast_dynamic-update-slice_fusion.2
  332.9 2.6 fusion.70
  344.1 2.3 bitcast_dynamic-update-slice_fusion.2
  350.5 2.6 fusion.70
  368.1 2.6 fusion.70
  379.5 2.3 bitcast_dynamic-update-slice_fusion.2
  385.8 2.5 fusion.70
  397.0 2.3 bitcast_dynamic-update-slice_fusion.2
  403.4 2.5 fusion.70
  414.5 2.3 bitcast_dynamic-update-slice_fusion.2
  420.9 2.5 fusion.70
  432.0 2.3 bitcast_dynamic-update-slice_fusion.2
  438.4 2.6 fusion.70
  449.6 2.3 bitcast_dynamic-update-slice_fusion.2
  456.0 2.6 fusion.70
  473.6 2.5 fusion.70
  491.2 2.5 fusion.70
  508.7 2.6 fusion.70
  526.3 2.6 fusion.70
  531.1 9.7 %slice.46 = f32[20,1152,128]{1,2,0:T(8,128)} slice(f32[20,1664,128]{1,2,0:T(8,128)} %get-tuple-element.70), slice={[0:20], [0:1152], [0:128]} | slice | bytes 23592960 | tf_op jit(solution)/shard_map/slice | solution.py:139
  540.9 9.7 %slice.45 = f32[20,1152,128]{1,2,0:T(8,128)} slice(f32[20,1664,128]{1,2,0:T(8,128)} %get-tuple-element.69), slice={[0:20], [0:1152], [0:128]} | slice | bytes 23592960 | tf_op jit(solution)/shard_map/slice | solution.py:139
  550.6 9.0 fusion.29
  559.6 3.6 fusion.44
  563.2 2.7 collective-permute-start.2
  565.9 5.4 collective-permute-start.3
  571.3 5.7 slice.53
  577.0 5.6 slice.52
  582.6 10.1 %pad_maximum_fusion.8 = f32[2,512,2560]{1,2,0:T(8,128)} fusion(f32[1,512,2560]{1,2,0:T(8,128)} %bitcast.170, f32[1,512,2560]{1,2,0:T(8,128)} %bitcast.171), kind=kLoop, calls=%fused_computation.47 | loop fusion | flops 2621440 | bytes 20971520 | tf_op jit(solution)/shard_map/stack | solution.py:138
  592.7 3.9 fusion.40
  596.7 57.5 %collective-permute-done.2 = bf16[2,384,2560]{1,2,0:T(8,128)(2,1)} collective-permute-done((bf16[2,384,2560]{1,2,0:T(8,128)(2,1)}, bf16[2,384,2560]{1,2,0:T(8,128)(2,1)}, u32[]{:S(2)}, u32[]{:S(2)}) %collective-permute-start.2) | collective-permute-done | bytes 3932192 | tf_op jit(solution)/shard_map/ppermute | solution.py:36
  655.4 5.0 fusion.32
  662.5 3.0 fusion.36
  666.9 235.2 %all-reduce.5 = bf16[2,512,2560]{1,2,0:T(8,128)(2,1)} all-reduce(f32[2,512,2560]{1,2,0:T(8,128)} %pad_maximum_fusion.8), channel_id=1, replica_groups=mesh['seq'=16,'section'=8] {'seq'}, use_global_device_ids=true, to_apply=%region_10.11 | all-reduce | flops 2621440 | bytes 15728640 | tf_op jit(solution)/shard_map/psum | solution.py:145
  902.2 2.4 copy.60
  904.6 7.9 copy.62
  912.5 4.0 copy.61
  (398 shorter events, 279.3 us)
Async XLA Ops:
  7.2 26.9 %copy-start = (s32[48,7]{0,1:T(8,128)S(1)}, s32[48,7]{0,1:T(8,128)}, u32[]{:S(2)}) copy-start(s32[48,7]{0,1:T(8,128)} %param.14) | copy-start | bytes 4036
  7.2 3.4 copy-start.7
  7.2 167.4 %all-reduce.4.cloned.1.call-start = ((), (), s32[]{:S(2)}) async-start(), calls=%async_computation | async-start | bytes 10485760 | tf_op jit(solution)/shard_map/psum | solution.py:30
  11.1 1.3 copy-start.2
  14.7 120.7 %collective-permute-start.1 = (bf16[2,384,2560]{1,2,0:T(8,128)(2,1)}, bf16[2,384,2560]{1,2,0:T(8,128)(2,1)}, u32[]{:S(2)}, u32[]{:S(2)}) collective-permute-start(bf16[2,384,2560]{1,2,0:T(8,128)(2,1)} %pad_maximum_fusion.9), channel_id=1, source_target_pairs={{8,0},{16,8},{24,16},{32,24},{40,32},{48,40},{56,48},{64,56},{72,6... | collective-permute-start | bytes 11796488 | tf_op jit(solution)/shard_map/ppermute | solution.py:21
  17.4 121.1 %collective-permute-start = (bf16[2,384,2560]{1,2,0:T(8,128)(2,1)}, bf16[2,384,2560]{1,2,0:T(8,128)(2,1)}, u32[]{:S(2)}, u32[]{:S(2)}) collective-permute-start(bf16[2,384,2560]{1,2,0:T(8,128)(2,1)} %pad_maximum_fusion.9), channel_id=1, source_target_pairs={{0,8},{8,16},{16,24},{24,32},{32,40},{40,48},{48,56},{56,64},{64,7... | collective-permute-start | bytes 11796488 | tf_op jit(solution)/shard_map/ppermute | solution.py:19
  34.0 0.7 copy-start.8
  38.7 99.8 %copy-start.3 = (bf16[1,384,2560]{1,2,0:T(8,128)(2,1)S(1)}, bf16[1,384,2560]{1,2,0:T(8,128)(2,1)}, u32[]{:S(2)}) copy-start(bf16[1,384,2560]{1,2,0:T(8,128)(2,1)} %copy-done.2) | copy-start | bytes 5898244
  185.6 3.9 copy-start.5
  203.1 3.9 copy-start.5
  220.7 3.9 copy-start.5
  238.2 3.9 copy-start.5
  255.7 3.9 copy-start.5
  273.3 3.9 copy-start.5
  290.8 3.9 copy-start.5
  308.3 3.9 copy-start.5
  325.9 3.9 copy-start.5
  343.4 3.9 copy-start.5
  361.1 3.9 copy-start.5
  378.8 3.9 copy-start.5
  396.3 3.9 copy-start.5
  413.8 3.9 copy-start.5
  431.4 3.9 copy-start.5
  448.9 3.9 copy-start.5
  466.6 3.9 copy-start.5
  484.1 3.9 copy-start.5
  501.7 3.9 copy-start.5
  519.3 3.9 copy-start.5
  563.2 91.0 %collective-permute-start.2 = (bf16[2,384,2560]{1,2,0:T(8,128)(2,1)}, bf16[2,384,2560]{1,2,0:T(8,128)(2,1)}, u32[]{:S(2)}, u32[]{:S(2)}) collective-permute-start(bf16[2,384,2560]{1,2,0:T(8,128)(2,1)} %get-tuple-element.175), channel_id=1, source_target_pairs={{8,0},{16,8},{24,16},{32,24},{40,32},{48,40},{56,48},{64,56},{72,6... | collective-permute-start | bytes 11796488 | tf_op jit(solution)/shard_map/ppermute | solution.py:36
  565.9 89.4 %collective-permute-start.3 = (bf16[2,384,2560]{1,2,0:T(8,128)(2,1)}, bf16[2,384,2560]{1,2,0:T(8,128)(2,1)}, u32[]{:S(2)}, u32[]{:S(2)}) collective-permute-start(bf16[2,384,2560]{1,2,0:T(8,128)(2,1)} %get-tuple-element.176), channel_id=1, source_target_pairs={{0,8},{8,16},{16,24},{24,32},{32,40},{40,48},{48,56},{56,64},{64,7... | collective-permute-start | bytes 11796488 | tf_op jit(solution)/shard_map/ppermute | solution.py:36
  582.6 72.8 %slice-start = ((s8[11796480]{0:T(1024)(128)(4,1)}), s8[4194304]{0:T(1024)(128)(4,1)S(1)}, s32[]{:S(2)}) async-start(s8[11796480]{0:T(1024)(128)(4,1)} %bitcast.162), calls=%async_computation.1 | async-start | bytes 8388608
  582.6 72.8 %slice-start.1 = ((s8[11796480]{0:T(1024)(128)(4,1)}), s8[4194304]{0:T(1024)(128)(4,1)S(1)}, s32[]{:S(2)}) async-start(s8[11796480]{0:T(1024)(128)(4,1)} %bitcast.162), calls=%async_computation.2 | async-start | bytes 8388608
  582.6 72.8 %slice-start.2 = ((s8[11796480]{0:T(1024)(128)(4,1)}), s8[3407872]{0:T(1024)(128)(4,1)S(1)}, s32[]{:S(2)}) async-start(s8[11796480]{0:T(1024)(128)(4,1)} %bitcast.162), calls=%async_computation.3 | async-start | bytes 6815744
  660.4 2.1 copy-start.4
  665.5 236.7 %copy-start.6 = (bf16[20,384,128]{1,2,0:T(8,128)(2,1)S(1)}, bf16[20,384,128]{1,2,0:T(8,128)(2,1)}, u32[]{:S(2)}) copy-start(bf16[20,384,128]{1,2,0:T(8,128)(2,1)} %get-tuple-element.68) | copy-start | bytes 5898244
  665.5 247.0 %collective-permute-start.4 = (bf16[384,2560]{0,1:T(8,128)(2,1)}, bf16[384,2560]{0,1:T(8,128)(2,1)}, u32[]{:S(2)}, u32[]{:S(2)}) collective-permute-start(bf16[384,2560]{0,1:T(8,128)(2,1)} %fusion.36), channel_id=1, source_target_pairs={{1,0},{2,1},{3,2},{4,3},{5,4},{6,5},{7,6},{9,8},{10,9},{11,10},{12... | collective-permute-start | bytes 5898248 | tf_op jit(solution)/shard_map/ppermute | solution.py:36
  904.6 11.9 %copy-start.1 = (s32[48,7]{0,1:T(8,128)S(1)}, s32[48,7]{0,1:T(8,128)}, u32[]{:S(2)}) copy-start(s32[48,7]{0,1:T(8,128)} %param.14) | copy-start | bytes 4036
Sparse Core Ops, SparseCore 0:
  34.2 140.4 all-reduce.3
where the time goes:
time: 929 us; the launch traced here: 923 us
  matrix products  237 us (26%)
  blocking collectives  235 us (25%)
  waiting for transfers between devices  181 us (19%)
  local copies, waits for them, and re-layouts  158 us (17%)
  other arithmetic  78.9 us (8%)
  starting transfers between devices  17.5 us (2%)
  between operations  14.9 us (2%)
    psum x1, blocking collectives, local(): text_total = lax.psum(dtext_part, 'seq')  235 us
    ppermute x1, waiting for transfers between devices, extended(): lax.ppermute(head, axis, [((i + 1) % count, i) for i in range(ends)])  93.5 us
    dynamic_slice x120, local copies, waits for them, and re-layouts, local(): lax.map(each_head_value, (divide_heads(normed_query), divide_heads(near[0...  68.1 us
    ppermute x3, waiting for transfers between devices, shifted(): return lax.ppermute(x, axis, pairs)  58.7 us
    dot_general x20, matrix products, query_side(): dvals = jnp.dot(probs_b.T, doh, preferred_element_type=jnp.float32)  51.2 us
    dot_general x20, matrix products, query_side(): out = jnp.dot(probs_b, vals, preferred_element_type=jnp.float32)  46 us
    dot_general x20, matrix products, query_side(): dkeys = jnp.dot(dscore.T, qh, preferred_element_type=jnp.float32)  44.5 us
    dot_general x20, matrix products, query_side(): dprob = jnp.dot(doh, vals.T, preferred_element_type=jnp.float32)  38.1 us
  transfers between devices with their start and end apart: 6, of which 5 were waited for; matrix products, arithmetic and copies ran while one was open for 7% of the time, Pallas kernels for 0%

commit v1 on v0

--- a/solution.py
+++ b/solution.py
@@ -142,7 +142,11 @@
         jnp.float32
     )
     own_rows = ext[:, token_rows : 2 * token_rows] + from_upper + from_lower
-    text_total = lax.psum(dtext_part, "seq")
+    text_total = dtext_part
+    for hop in (1, 2, 4, 8):
+        text_total = text_total + lax.ppermute(
+            text_total, "seq", [(dev, dev ^ hop) for dev in range(16)]
+        )
     grad_hidden = (
         own_rows[1]
         + norm_backward(

time: 929 us -> 1650 us (1.78); the launches traced: 923 us -> 1620 us
  waiting for transfers between devices: 181 us -> 1060 us
  blocking collectives: 235 us -> 0 us
  other arithmetic: 78.9 us -> 126 us
    ppermute x0 -> x4, waiting for transfers between devices: none -> 659 us  [local(): lax.ppermute(text_total, 'seq', [(dev, dev ^ hop) for dev in range(16)])]
    psum x1 -> x0, blocking collectives: 235 us -> none  [local(): text_total = lax.psum(dtext_part, 'seq')]
    ppermute x3, waiting for transfers between devices: 58.7 us -> 279 us  [shifted(): return lax.ppermute(x, axis, pairs)]
    add x0 -> x3, other arithmetic: none -> 39.4 us  [local(): text_total + lax.ppermute(text_total, 'seq', [(dev, dev ^ hop) for dev in...]
  transfers between devices with their start and end apart: 6 -> 10, of which waited for: 5 -> 8; matrix products, arithmetic and copies ran while one was open for 7% -> 5% of each run, Pallas kernels for 0% -> 0%
where the time goes in v1:
time: 1650 us; the launch traced here: 1620 us
  waiting for transfers between devices  1060 us (64%)
  matrix products  237 us (14%)
  local copies, waits for them, and re-layouts  158 us (10%)
  other arithmetic  126 us (8%)
  starting transfers between devices  21.7 us (1%)
    ppermute x4, waiting for transfers between devices, local(): lax.ppermute(text_total, 'seq', [(dev, dev ^ hop) for dev in range(16)])  659 us
    ppermute x3, waiting for transfers between devices, shifted(): return lax.ppermute(x, axis, pairs)  279 us
    ppermute x1, waiting for transfers between devices, extended(): lax.ppermute(head, axis, [((i + 1) % count, i) for i in range(ends)])  93.4 us
    dynamic_slice x120, local copies, waits for them, and re-layouts, local(): lax.map(each_head_value, (divide_heads(normed_query), divide_heads(near[0...  67.8 us
    dot_general x20, matrix products, query_side(): dvals = jnp.dot(probs_b.T, doh, preferred_element_type=jnp.float32)  51.2 us
    dot_general x20, matrix products, query_side(): out = jnp.dot(probs_b, vals, preferred_element_type=jnp.float32)  46 us
    dot_general x20, matrix products, query_side(): dkeys = jnp.dot(dscore.T, qh, preferred_element_type=jnp.float32)  44.5 us
    add x3, other arithmetic, local(): text_total + lax.ppermute(text_total, 'seq', [(dev, dev ^ hop) for dev in...  39.4 us
  transfers between devices with their start and end apart: 10, of which 8 were waited for; matrix products, arithmetic and copies ran while one was open for 5% of the time, Pallas kernels for 0%

profile of v1, /device:TPU:24, one launch (start us, length us, event | category | flops | bytes accessed | tf_op | source)
XLA Modules:
  0.0 1619.7 jit_solution(10605565059718131349)
XLA Ops:
  7.2 2.8 copy.43
  14.7 2.6 collective-permute-start.1
  17.4 5.3 collective-permute-start
  23.3 8.0 copy.45
  31.3 2.7 select_bitcast_fusion
  34.7 4.0 copy.46
  38.8 3.2 fusion.43
  42.0 93.4 %collective-permute-done.1 = bf16[2,384,2560]{1,2,0:T(8,128)(2,1)} collective-permute-done((bf16[2,384,2560]{1,2,0:T(8,128)(2,1)}, bf16[2,384,2560]{1,2,0:T(8,128)(2,1)}, u32[]{:S(2)}, u32[]{:S(2)}) %collective-permute-start.1) | collective-permute-done | bytes 3932192 | tf_op jit(solution)/shard_map/ppermute | solution.py:21
  135.4 3.1 collective-permute-done
  138.5 5.1 pad_maximum_fusion.7
  143.6 4.9 fusion.47
  148.5 26.0 %all-reduce.3.cloned.1.call-done = bf16[2,512,2560]{1,2,0:T(8,128)(2,1)} async-done(((bf16[2,512,2560]{1,2,0:T(8,128)(2,1)}), bf16[2,512,2560]{1,2,0:T(8,128)(2,1)}) %all-reduce.3.cloned.1.call-update) | async-done | bytes 5242896 | tf_op jit(solution)/shard_map/psum | solution.py:30
  174.6 5.2 fusion.48
  179.8 351.1 %while.17 = (s32[]{:T(128)}, bf16[20,384,128]{1,2,0:T(8,128)(2,1)}, f32[20,384,128]{1,2,0:T(8,128)}, f32[20,1664,128]{1,2,0:T(8,128)}, f32[20,1664,128]{1,2,0:T(...) while((s32[]{:T(128)}, bf16[20,384,128]{1,2,0:T(8,128)(2,1)}, ...), condition=%wide.region_7.8_spmd.clone, body=%wide.region_3.7_spmd.clone.sunk | while | flops 996523264 | bytes 28792892 | solution.py:125
  192.6 2.5 fusion.73
  203.7 2.3 bitcast_dynamic-update-slice_fusion.2
  210.1 2.6 fusion.73
  227.7 2.5 fusion.73
  238.8 2.3 bitcast_dynamic-update-slice_fusion.2
  245.2 2.5 fusion.73
  256.3 2.3 bitcast_dynamic-update-slice_fusion.2
  262.7 2.6 fusion.73
  280.2 2.6 fusion.73
  291.4 2.3 bitcast_dynamic-update-slice_fusion.2
  297.8 2.5 fusion.73
  315.3 2.6 fusion.73
  332.9 2.5 fusion.73
  344.0 2.3 bitcast_dynamic-update-slice_fusion.2
  350.4 2.6 fusion.73
  353.0 2.3 fusion.72
  368.1 2.6 fusion.73
  370.7 2.3 fusion.72
  385.7 2.6 fusion.73
  403.3 2.5 fusion.73
  420.8 2.5 fusion.73
  438.3 2.6 fusion.73
  449.5 2.3 bitcast_dynamic-update-slice_fusion.2
  455.8 2.5 fusion.73
  473.4 2.5 fusion.73
  491.0 2.6 fusion.73
  508.5 2.6 fusion.73
  526.1 2.5 fusion.73
  530.9 3.3 slice.53
  534.2 5.2 slice.52
  539.5 5.5 pad_maximum_fusion.8
  545.8 226.6 %collective-permute-done.5 = f32[2,512,2560]{1,2,0:T(8,128)} collective-permute-done((f32[2,512,2560]{1,2,0:T(8,128)}, f32[2,512,2560]{1,2,0:T(8,128)}, u32[]{:S(2)}, u32[]{:S(2)}) %collective-permute-start.5) | collective-permute-done | bytes 10485792 | tf_op jit(solution)/shard_map/ppermute | solution.py:147
  772.5 13.6 fusion.44
  787.5 226.6 %collective-permute-done.6 = f32[2,512,2560]{1,2,0:T(8,128)S(1)} collective-permute-done((f32[2,512,2560]{1,2,0:T(8,128)}, f32[2,512,2560]{1,2,0:T(8,128)S(1)}, u32[]{:S(2)}, u32[]{:S(2)}) %collective-permute-start.6) | collective-permute-done | bytes 10485792 | tf_op jit(solution)/shard_map/ppermute | solution.py:147
  1014.1 12.4 fusion.51
  1026.7 9.7 slice.46
  1036.4 9.8 slice.45
  1046.3 205.8 %collective-permute-done.7 = f32[2,512,2560]{1,2,0:T(8,128)} collective-permute-done((f32[2,512,2560]{1,2,0:T(8,128)}, f32[2,512,2560]{1,2,0:T(8,128)}, u32[]{:S(2)}, u32[]{:S(2)}) %collective-permute-start.7) | collective-permute-done | bytes 10485792 | tf_op jit(solution)/shard_map/ppermute | solution.py:147
  1252.1 13.4 add.71
  1267.0 14.7 fusion.29
  1281.7 6.6 fusion.46
  1288.3 3.3 collective-permute-start.2
  1291.6 5.2 collective-permute-start.3
  1297.5 278.6 %collective-permute-done.2 = bf16[2,384,2560]{1,2,0:T(8,128)(2,1)} collective-permute-done((bf16[2,384,2560]{1,2,0:T(8,128)(2,1)}, bf16[2,384,2560]{1,2,0:T(8,128)(2,1)}, u32[]{:S(2)}, u32[]{:S(2)}) %collective-permute-start.2) | collective-permute-done | bytes 3932192 | tf_op jit(solution)/shard_map/ppermute | solution.py:36
  1576.2 4.0 fusion.32
  1582.3 3.0 fusion.37
  1586.6 4.0 copy.60
  1591.4 2.4 copy.61
  1593.8 11.2 fusion.33
  1604.9 7.9 copy.62
  (426 shorter events, 294.8 us)
Async XLA Ops:
  7.2 26.8 %copy-start = (s32[48,7]{0,1:T(8,128)S(1)}, s32[48,7]{0,1:T(8,128)}, u32[]{:S(2)}) copy-start(s32[48,7]{0,1:T(8,128)} %param.14) | copy-start | bytes 4036
  7.2 3.4 copy-start.12
  7.2 167.4 %all-reduce.3.cloned.1.call-start = ((), (), s32[]{:S(2)}) async-start(), calls=%async_computation | async-start | bytes 10485760 | tf_op jit(solution)/shard_map/psum | solution.py:30
  10.6 4.1 copy-start.10
  11.2 1.3 copy-start.4
  14.7 120.7 %collective-permute-start.1 = (bf16[2,384,2560]{1,2,0:T(8,128)(2,1)}, bf16[2,384,2560]{1,2,0:T(8,128)(2,1)}, u32[]{:S(2)}, u32[]{:S(2)}) collective-permute-start(bf16[2,384,2560]{1,2,0:T(8,128)(2,1)} %pad_maximum_fusion.9), channel_id=1, source_target_pairs={{8,0},{16,8},{24,16},{32,24},{40,32},{48,40},{56,48},{64,56},{72,6... | collective-permute-start | bytes 11796488 | tf_op jit(solution)/shard_map/ppermute | solution.py:21
  17.4 121.1 %collective-permute-start = (bf16[2,384,2560]{1,2,0:T(8,128)(2,1)}, bf16[2,384,2560]{1,2,0:T(8,128)(2,1)}, u32[]{:S(2)}, u32[]{:S(2)}) collective-permute-start(bf16[2,384,2560]{1,2,0:T(8,128)(2,1)} %pad_maximum_fusion.9), channel_id=1, source_target_pairs={{0,8},{8,16},{16,24},{24,32},{32,40},{40,48},{48,56},{56,64},{64,7... | collective-permute-start | bytes 11796488 | tf_op jit(solution)/shard_map/ppermute | solution.py:19
  34.0 0.7 copy-start.13
  38.7 99.7 %copy-start.5 = (bf16[1,384,2560]{1,2,0:T(8,128)(2,1)S(1)}, bf16[1,384,2560]{1,2,0:T(8,128)(2,1)}, u32[]{:S(2)}) copy-start(bf16[1,384,2560]{1,2,0:T(8,128)(2,1)} %copy-done.4) | copy-start | bytes 5898244
  185.5 3.9 copy-start.9
  203.0 3.9 copy-start.9
  220.6 3.9 copy-start.9
  238.2 3.9 copy-start.9
  255.6 3.9 copy-start.9
  273.2 3.9 copy-start.9
  290.7 3.9 copy-start.9
  308.3 3.9 copy-start.9
  325.8 3.9 copy-start.9
  343.3 3.9 copy-start.9
  361.0 3.9 copy-start.9
  378.7 3.9 copy-start.9
  396.2 3.9 copy-start.9
  413.7 3.9 copy-start.9
  431.2 3.9 copy-start.9
  448.8 3.9 copy-start.9
  466.4 3.9 copy-start.9
  483.9 3.9 copy-start.9
  501.5 3.9 copy-start.9
  519.1 3.9 copy-start.9
  534.2 5.3 copy-start.2
  539.5 5.5 copy-start.3
  545.0 227.5 %collective-permute-start.5 = (f32[2,512,2560]{1,2,0:T(8,128)}, f32[2,512,2560]{1,2,0:T(8,128)}, u32[]{:S(2)}, u32[]{:S(2)}) collective-permute-start(f32[2,512,2560]{1,2,0:T(8,128)} %pad_maximum_fusion.8), channel_id=1, source_target_pairs={{0,8},{8,0},{16,24},{24,16},{32,40},{40,32},{48,56},{56,48},{64,72... | collective-permute-start | bytes 31457288 | tf_op jit(solution)/shard_map/ppermute | solution.py:147
  786.1 228.0 %collective-permute-start.6 = (f32[2,512,2560]{1,2,0:T(8,128)}, f32[2,512,2560]{1,2,0:T(8,128)S(1)}, u32[]{:S(2)}, u32[]{:S(2)}) collective-permute-start(f32[2,512,2560]{1,2,0:T(8,128)} %fusion.44), channel_id=1, source_target_pairs={{0,16},{8,24},{16,0},{24,8},{32,48},{40,56},{48,32},{56,40},{64,80... | collective-permute-start | bytes 31457288 | tf_op jit(solution)/shard_map/ppermute | solution.py:147
  1026.4 225.7 %collective-permute-start.7 = (f32[2,512,2560]{1,2,0:T(8,128)}, f32[2,512,2560]{1,2,0:T(8,128)}, u32[]{:S(2)}, u32[]{:S(2)}) collective-permute-start(f32[2,512,2560]{1,2,0:T(8,128)} %fusion.51), channel_id=1, source_target_pairs={{0,32},{8,40},{16,48},{24,56},{32,0},{40,8},{48,16},{56,24},{64,96... | collective-permute-start | bytes 31457288 | tf_op jit(solution)/shard_map/ppermute | solution.py:147
  1265.5 328.3 %collective-permute-start.8 = (f32[2,512,2560]{1,2,0:T(8,128)}, f32[2,512,2560]{1,2,0:T(8,128)}, u32[]{:S(2)}, u32[]{:S(2)}) collective-permute-start(f32[2,512,2560]{1,2,0:T(8,128)} %add.71), channel_id=1, source_target_pairs={{0,64},{8,72},{16,80},{24,88},{32,96},{40,104},{48,112},{56,120},{... | collective-permute-start | bytes 31457288 | tf_op jit(solution)/shard_map/ppermute | solution.py:147
  1267.0 29.8 %copy-start.8 = (f32[384,20,128]{0,2,1:T(8,128)S(1)}, f32[384,20,128]{0,2,1:T(8,128)}, u32[]{:S(2)}) copy-start(f32[384,20,128]{0,2,1:T(8,128)} %get-tuple-element.166) | copy-start | bytes 11796484
  1267.0 309.1 %slice-start.3 = ((s8[11796480]{0:T(1024)(128)(4,1)}), s8[4194304]{0:T(1024)(128)(4,1)S(1)}, s32[]{:S(2)}) async-start(s8[11796480]{0:T(1024)(128)(4,1)} %bitcast.165), calls=%async_computation.4 | async-start | bytes 8388608
  1267.0 309.1 %slice-start.4 = ((s8[11796480]{0:T(1024)(128)(4,1)}), s8[4194304]{0:T(1024)(128)(4,1)S(1)}, s32[]{:S(2)}) async-start(s8[11796480]{0:T(1024)(128)(4,1)} %bitcast.165), calls=%async_computation.5 | async-start | bytes 8388608
  1281.7 15.1 copy-start.6
  1281.7 294.4 %slice-start = ((s8[11796480]{0:T(1024)(128)(4,1)}), s8[4194304]{0:T(1024)(128)(4,1)S(1)}, s32[]{:S(2)}) async-start(s8[11796480]{0:T(1024)(128)(4,1)} %bitcast.161), calls=%async_computation.1 | async-start | bytes 8388608
  1281.7 294.4 %slice-start.1 = ((s8[11796480]{0:T(1024)(128)(4,1)}), s8[4194304]{0:T(1024)(128)(4,1)S(1)}, s32[]{:S(2)}) async-start(s8[11796480]{0:T(1024)(128)(4,1)} %bitcast.161), calls=%async_computation.2 | async-start | bytes 8388608
  1281.7 294.4 %slice-start.5 = ((s8[11796480]{0:T(1024)(128)(4,1)}), s8[3407872]{0:T(1024)(128)(4,1)S(1)}, s32[]{:S(2)}) async-start(s8[11796480]{0:T(1024)(128)(4,1)} %bitcast.165), calls=%async_computation.6 | async-start | bytes 6815744
  1288.3 287.7 %collective-permute-start.2 = (bf16[2,384,2560]{1,2,0:T(8,128)(2,1)}, bf16[2,384,2560]{1,2,0:T(8,128)(2,1)}, u32[]{:S(2)}, u32[]{:S(2)}) collective-permute-start(bf16[2,384,2560]{1,2,0:T(8,128)(2,1)} %get-tuple-element.175), channel_id=1, source_target_pairs={{8,0},{16,8},{24,16},{32,24},{40,32},{48,40},{56,48},{64,56},{72,6... | collective-permute-start | bytes 11796488 | tf_op jit(solution)/shard_map/ppermute | solution.py:36
  1291.6 284.5 %collective-permute-start.3 = (bf16[2,384,2560]{1,2,0:T(8,128)(2,1)}, bf16[2,384,2560]{1,2,0:T(8,128)(2,1)}, u32[]{:S(2)}, u32[]{:S(2)}) collective-permute-start(bf16[2,384,2560]{1,2,0:T(8,128)(2,1)} %get-tuple-element.176), channel_id=1, source_target_pairs={{0,8},{8,16},{16,24},{24,32},{32,40},{40,48},{48,56},{56,64},{64,7... | collective-permute-start | bytes 11796488 | tf_op jit(solution)/shard_map/ppermute | solution.py:36
  1296.8 279.3 %slice-start.2 = ((s8[11796480]{0:T(1024)(128)(4,1)}), s8[3407872]{0:T(1024)(128)(4,1)S(1)}, s32[]{:S(2)}) async-start(s8[11796480]{0:T(1024)(128)(4,1)} %bitcast.161), calls=%async_computation.3 | async-start | bytes 6815744
  1297.4 282.7 %copy-start.11 = (f32[2560]{0:T(1024)S(1)}, f32[2560]{0:T(1024)}, u32[]{:S(2)}) copy-start(f32[2560]{0:T(1024)} %copy-done.10) | copy-start | bytes 30724
  1580.2 2.1 copy-start.7
  1585.3 6.1 collective-permute-start.4
  1593.8 19.1 %copy-start.1 = (s32[48,7]{0,1:T(8,128)S(1)}, s32[48,7]{0,1:T(8,128)}, u32[]{:S(2)}) copy-start(s32[48,7]{0,1:T(8,128)} %param.14) | copy-start | bytes 4036
Sparse Core Ops, SparseCore 0:
  34.1 140.4 all-reduce.2
